TPU v7x, 512 devices: a whole 4x8x8 slice. The times are simulated.
512 devices in a mesh: island: 16 (over y, core), fsdp: 32 (over z, x).
Axes of the slice: x: 4, y: 8, z: 8, core: 2. Of those that a mesh axis runs over, the one named last changes fastest.
Arguments:
- delta: bfloat16 [16, 2048, 4096], P('island', 'fsdp'), may hold values from -6 to 6
- error: float32 [16, 2048, 4096], P('island', 'fsdp'), may hold values from -6 to 6
- param: bfloat16 [2048, 4096], P('fsdp'), may hold values from -6 to 6
- velocity: bfloat16 [2048, 4096], P('fsdp'), may hold values from -4 to 4
- piece_ids: int32 [32, 32, 16], P('fsdp'), may hold values from 0 to 2047, as said below
- piece_counts: int32 [32, 32], P('fsdp'), may hold values from 8 to 16, as said below
Outputs:
- new_error: float32 [16, 2048, 4096], P('island', 'fsdp')
- new_param: bfloat16 [2048, 4096], P('fsdp')
- new_velocity: bfloat16 [2048, 4096], P('fsdp')
- compressed: float32 [32, 32, 16, 128], P('fsdp')
Inputs may be any that keep to these rules, and one draw needn't show every extreme that they name: `piece_ids`: within one shard's lists all entries are distinct, entries past the count included; those are ignored. `piece_counts`: one owner receives exactly 16 live entries from every shard.
All inputs are finite; a program needn't handle non-finite values.
Results may differ from a plain program's by a relative error of at most 0.001.
Values sent between devices are 32-bit elements; how exact they have to be, the bound alone decides.
A program may use at most 64 MiB of HBM per device.

v0:
```python
import jax
import jax.numpy as jnp
from jax import lax
from jax.sharding import PartitionSpec as P

decay_rate = 0.9
outer_rate = 0.7
nesterov = 0.9
eps_value = 1e-06


def cosine_table(side):
    freq = jnp.arange(side, dtype=jnp.int32)[:, None].astype(jnp.float32)
    place = jnp.arange(side, dtype=jnp.int32)[None, :].astype(jnp.float32)
    scale = jnp.where(freq == 0.0, jnp.sqrt(1.0 / side), jnp.sqrt(2.0 / side))
    return scale * jnp.cos(jnp.pi * (2.0 * place + 1.0) * freq / (2.0 * side))


def transform(field, table, column_table):
    rows, width = field.shape
    side = table.shape[0]
    right = jnp.dot(field.reshape(-1, 128), column_table, precision=lax.Precision.HIGHEST)
    right = right.reshape(rows // side, side, width // 128, 128)
    left = jnp.einsum("kn,rnqj->rqkj", table, right, precision=lax.Precision.HIGHEST)
    return left.reshape(-1, 128)


def inverse(pieces, table, column_table, rows, width):
    side = table.shape[0]
    blocks = pieces.reshape(rows // side, width // 128, side, 128)
    left = jnp.einsum("kn,rqkj->rnqj", table, blocks, precision=lax.Precision.HIGHEST)
    back = jnp.dot(left.reshape(-1, 128), column_table.T, precision=lax.Precision.HIGHEST)
    return back.reshape(rows, width)


def normalize(values):
    return values / jnp.sqrt(jnp.mean(values * values, axis=-1, keepdims=True) + eps_value)


def island_norm(pieces):
    total = lax.psum(pieces, "island")
    return normalize(total)


def shards(delta, error, param, velocity, piece_ids, piece_counts):
    rows, width = param.shape
    table = cosine_table(64)
    column_table = jnp.kron(jnp.eye(2, dtype=jnp.float32), table.T)
    momentum = decay_rate * error[0] + delta[0].astype(jnp.float32)
    coefficients = transform(momentum, table, column_table)
    piece_list = piece_ids[0]
    owners, slots = piece_list.shape
    slot_index = jnp.arange(slots, dtype=jnp.int32)[None, :]
    active = (slot_index < piece_counts[0][:, None]).astype(jnp.float32)
    chosen = coefficients[piece_list] * active[..., None]
    flat_ids = piece_list.reshape(-1)
    arrived = lax.all_to_all(chosen, "fsdp", split_axis=0, concat_axis=0, tiled=True)
    compressed = island_norm(arrived)
    returned = lax.all_to_all(compressed, "fsdp", split_axis=0, concat_axis=0, tiled=True)
    kept_mask = (
        jnp.zeros((coefficients.shape[0],), jnp.float32).at[flat_ids].set(active.reshape(-1))
    )
    new_error = momentum - inverse(
        coefficients * kept_mask[:, None], table, column_table, rows, width
    )
    scattered = (
        jnp.zeros(coefficients.shape, jnp.float32).at[flat_ids].add(returned.reshape(-1, 128))
    )
    update = inverse(scattered, table, column_table, rows, width)
    moved = nesterov * velocity.astype(jnp.float32) + update
    new_velocity = moved.astype(jnp.bfloat16)
    new_param = (param.astype(jnp.float32) - outer_rate * (update + nesterov * moved)).astype(
        jnp.bfloat16
    )
    return (new_error[None], new_param, new_velocity, compressed[None])


def solution(mesh):
    in_specs = (
        P("island", "fsdp", None),
        P("island", "fsdp", None),
        P("fsdp", None),
        P("fsdp", None),
        P("fsdp", None, None),
        P("fsdp", None),
    )
    out_specs = (
        P("island", "fsdp", None),
        P("fsdp", None),
        P("fsdp", None),
        P("fsdp", None, None, None),
    )
    return jax.shard_map(shards, mesh=mesh, in_specs=in_specs, out_specs=out_specs, check_vma=False)
```

profile of v0, /device:TPU:24, one launch (start us, length us, event | category | flops | bytes accessed | tf_op | source)
XLA Modules:
  0.0 192.9 jit_solution(322883646928115541)
XLA Ops:
  7.2 0.8 compare_select_fusion
  8.0 0.1 copy.16
  8.0 0.1 reshape.265
  8.1 0.7 fusion.26
  8.9 0.2 cosine_multiply_fusion.4
  9.1 0.1 copy.12
  9.1 0.1 broadcast_multiply_fusion.1
  9.3 0.1 reshape.288
  9.4 1.3 fusion.6
  10.7 0.2 copy.21
  10.9 1.6 fusion.2
  12.6 1.2 fusion.12
  13.8 1.0 gather_fusion
  14.8 0.8 broadcast_multiply_fusion
  15.7 13.2 %all-to-all-start = ((f32[32,16,128]{2,1,0:T(8,128)}), f32[32,16,128]{2,1,0:T(8,128)S(1)}, u32[]{:S(2)}, u32[]{:S(2)}) async-start(f32[32,16,128]{2,1,0:T(8,128)} %broadcast_multiply_fusion), calls=%async_computation | async-start | bytes 524288 | tf_op jit(solution)/shard_map/all_to_all | solution.py:57
  28.9 0.0 copy-start.6
  28.9 0.0 all-reduce.2.cloned.1.call-start
  28.9 0.1 reshape.275
  29.0 0.6 copy-done.6
  29.6 0.1 copy.14
  29.6 0.1 mul.231
  29.8 0.1 reshape_squeeze.3
  29.8 2.5 %scatter_custom_fusion = f32[2048]{0:T(1024)S(1)} fusion(s32[512]{0:T(512)S(1)} %bitcast.60, f32[512]{0:T(512)S(1)} %reshape.275, f32[]{:T(128)} %constant.13.clone.1), kind=kCustom, calls=%fused_computation.46 | custom fusion | bytes 8196 | tf_op jit(solution)/shard_map/scatter | solution.py:61
  32.3 0.1 mul.237
  32.4 1.3 convolution_bitcast_fusion.1
  33.7 0.6 copy.15
  34.3 7.2 %all-to-all-done = f32[32,16,128]{2,1,0:T(8,128)S(1)} async-done(((f32[32,16,128]{2,1,0:T(8,128)}), f32[32,16,128]{2,1,0:T(8,128)S(1)}, u32[]{:S(2)}, u32[]{:S(2)}) %all-to-all-start) | async-done | bytes 262176 | tf_op jit(solution)/shard_map/all_to_all | solution.py:57
  41.5 0.7 copy-done.3
  42.2 0.0 all-reduce.2.cloned.1.call-update
  42.3 1.0 fusion.32
  43.3 0.2 reshape.256
  43.5 0.0 copy-start
  43.5 107.5 %all-reduce.2.cloned.1.call-done = f32[32,16,128]{2,1,0:T(8,128)} async-done(((f32[32,16,128]{2,1,0:T(8,128)}), f32[32,16,128]{2,1,0:T(8,128)}) %all-reduce.2.cloned.1.call-update) | async-done | bytes 262160 | tf_op jit(solution)/shard_map/psum | solution.py:41
  151.0 1.1 multiply_reduce_fusion
  152.1 1.8 broadcast_divide_fusion
  153.9 10.2 %all-to-all-start.1 = ((f32[32,16,128]{2,1,0:T(8,128)}), f32[32,16,128]{2,1,0:T(8,128)S(1)}, u32[]{:S(2)}, u32[]{:S(2)}) async-start(f32[32,16,128]{2,1,0:T(8,128)} %broadcast_divide_fusion), calls=%async_computation.1 | async-start | bytes 524288 | tf_op jit(solution)/shard_map/all_to_all | solution.py:59
  164.1 1.1 fusion.5
  165.3 0.8 fusion.41
  166.1 11.9 %all-to-all-done.1 = f32[32,16,128]{2,1,0:T(8,128)S(1)} async-done(((f32[32,16,128]{2,1,0:T(8,128)}), f32[32,16,128]{2,1,0:T(8,128)S(1)}, u32[]{:S(2)}, u32[]{:S(2)}) %all-to-all-start.1) | async-done | bytes 262176 | tf_op jit(solution)/shard_map/all_to_all | solution.py:59
  178.0 2.7 %scatter_custom_fusion.1 = f32[2048,128]{1,0:T(8,128)S(1)} fusion(s32[512]{0:T(512)S(1)} %bitcast.61, f32[512,128]{1,0:T(8,128)S(1)} %bitcast.59, f32[]{:T(128)} %constant.13.clone.1), kind=kCustom, calls=%fused_computation.15 | custom fusion | flops 65536 | bytes 1048580 | tf_op jit(solution)/shard_map/scatter-add | solution.py:67
  180.6 1.3 convolution_bitcast_fusion
  181.9 0.6 copy.17
  182.5 1.0 fusion.33
  183.5 0.0 copy-start.4
  183.6 0.2 reshape.261
  183.8 0.8 copy-done.4
  184.6 0.2 copy-done.5
  184.7 1.3 fusion.4
  (13 shorter events, 0.1 us)
Async XLA Ops:
  7.2 2.2 %copy-start.2 = (bf16[1,64,4096]{2,1,0:T(8,128)(2,1)S(1)}, bf16[1,64,4096]{2,1,0:T(8,128)(2,1)}, u32[]{:S(2)}) copy-start(bf16[1,64,4096]{2,1,0:T(8,128)(2,1)} %param.6) | copy-start | bytes 1572868
  15.7 25.9 %all-to-all-start = ((f32[32,16,128]{2,1,0:T(8,128)}), f32[32,16,128]{2,1,0:T(8,128)S(1)}, u32[]{:S(2)}, u32[]{:S(2)}) async-start(f32[32,16,128]{2,1,0:T(8,128)} %broadcast_multiply_fusion), calls=%async_computation | async-start | bytes 524288 | tf_op jit(solution)/shard_map/all_to_all | solution.py:57
  28.9 0.7 copy-start.6
  28.9 122.1 %all-reduce.2.cloned.1.call-start = ((), (), s32[]{:S(2)}) async-start(), calls=%async_computation.2 | async-start | bytes 524288 | tf_op jit(solution)/shard_map/psum | solution.py:41
  41.5 0.7 copy-start.3
  43.5 120.7 %copy-start = (f32[1,64,4096]{2,1,0:T(8,128)S(1)}, f32[1,64,4096]{2,1,0:T(8,128)}, u32[]{:S(2)}) copy-start(f32[1,64,4096]{2,1,0:T(8,128)} %param.7) | copy-start | bytes 3145732
  153.9 24.0 %all-to-all-start.1 = ((f32[32,16,128]{2,1,0:T(8,128)}), f32[32,16,128]{2,1,0:T(8,128)S(1)}, u32[]{:S(2)}, u32[]{:S(2)}) async-start(f32[32,16,128]{2,1,0:T(8,128)} %broadcast_divide_fusion), calls=%async_computation.1 | async-start | bytes 524288 | tf_op jit(solution)/shard_map/all_to_all | solution.py:59
  164.1 1.1 copy-start.1
  183.5 1.0 copy-start.4
  183.6 1.2 copy-start.5
Sparse Core Ops, SparseCore 0:
  42.4 108.5 all-reduce.1
where the time goes:
time: 193 us
  waiting for transfers between devices  127 us (66%)
  starting transfers between devices  23.4 us (12%)
  between operations  14.3 us (7%)
  other arithmetic  12.8 us (7%)
  local copies, waits for them, and re-layouts  8.35 us (4%)
  matrix products  7.44 us (4%)
    psum x1, waiting for transfers between devices, island_norm(): total = lax.psum(pieces, 'island')  108 us
    all_to_all x1, starting transfers between devices, shards(): lax.all_to_all(chosen, 'fsdp', split_axis=0, concat_axis=0, tiled=True)  13.2 us
    all_to_all x1, waiting for transfers between devices, shards(): lax.all_to_all(compressed, 'fsdp', split_axis=0, concat_axis=0, tiled=True)  11.9 us
    all_to_all x1, starting transfers between devices, shards(): lax.all_to_all(compressed, 'fsdp', split_axis=0, concat_axis=0, tiled=True)  10.2 us
    all_to_all x1, waiting for transfers between devices, shards(): lax.all_to_all(chosen, 'fsdp', split_axis=0, concat_axis=0, tiled=True)  7.21 us
  transfers between devices with their start and end apart: 3, of which 3 were waited for; matrix products, arithmetic and copies ran while one was open for 4% of the time, Pallas kernels for 0%

commit v1 on v0

--- a/solution.py
+++ b/solution.py
@@ -38,7 +38,10 @@
 
 
 def island_norm(pieces):
-    total = lax.psum(pieces, "island")
+    size, total = (lax.axis_size("island"), pieces)
+    for far in [1 << k for k in range(size.bit_length() - 1)]:
+        route = [(i, i ^ far) for i in range(size)]
+        total = total + lax.ppermute(total, "island", route)
     return normalize(total)
 
 

time: 193 us -> 109 us (0.56)
  waiting for transfers between devices: 127 us -> 41.2 us
  blocking collectives: 0 us -> 25.6 us
  between operations: 14.3 us -> 0.92 us
  starting transfers between devices: 23.4 us -> 16.1 us
  other arithmetic: 12.8 us -> 10.1 us
    psum x1 -> x0, waiting for transfers between devices: 108 us -> none  [island_norm(): total = lax.psum(pieces, 'island')]
    ppermute x0 -> x4, waiting for transfers between devices: none -> 30.4 us  [island_norm(): total = total + lax.ppermute(total, 'island', route)]
    all_to_all x0 -> x1, blocking collectives: none -> 25.6 us  [shards(): lax.all_to_all(chosen, 'fsdp', split_axis=0, concat_axis=0, tiled=True)]
    all_to_all x1 -> x0, starting transfers between devices: 13.2 us -> none  [shards(): lax.all_to_all(chosen, 'fsdp', split_axis=0, concat_axis=0, tiled=True)]
    ppermute x0 -> x4, starting transfers between devices: none -> 11.8 us  [island_norm(): total = total + lax.ppermute(total, 'island', route)]
    all_to_all x1 -> x0, waiting for transfers between devices: 7.21 us -> none  [shards(): lax.all_to_all(chosen, 'fsdp', split_axis=0, concat_axis=0, tiled=True)]
    all_to_all x1, starting transfers between devices: 10.2 us -> 4.27 us  [shards(): lax.all_to_all(compressed, 'fsdp', split_axis=0, concat_axis=0, tiled=True)]
  transfers between devices with their start and end apart: 3 -> 5, of which waited for: 3 -> 5; matrix products, arithmetic and copies ran while one was open for 4% -> 7% of each run, Pallas kernels for 0% -> 0%
where the time goes in v1:
time: 109 us; the launch traced here: 108 us
  waiting for transfers between devices  41.2 us (38%)
  blocking collectives  25.6 us (23%)
  starting transfers between devices  16.1 us (15%)
  other arithmetic  10.1 us (9%)
  matrix products  7.44 us (7%)
  local copies, waits for them, and re-layouts  7.08 us (6%)
    ppermute x4, waiting for transfers between devices, island_norm(): total = total + lax.ppermute(total, 'island', route)  30.4 us
    all_to_all x1, blocking collectives, shards(): lax.all_to_all(chosen, 'fsdp', split_axis=0, concat_axis=0, tiled=True)  25.6 us
    ppermute x4, starting transfers between devices, island_norm(): total = total + lax.ppermute(total, 'island', route)  11.8 us
    all_to_all x1, waiting for transfers between devices, shards(): lax.all_to_all(compressed, 'fsdp', split_axis=0, concat_axis=0, tiled=True)  10.9 us
    all_to_all x1, starting transfers between devices, shards(): lax.all_to_all(compressed, 'fsdp', split_axis=0, concat_axis=0, tiled=True)  4.27 us
    dot_general x2, matrix products, inverse(): jnp.einsum('kn,rqkj->rnqj', table, blocks, precision=lax.Precision.HIGHEST)  2.6 us
    scatter-add x1, other arithmetic, shards(): jnp.zeros(coefficients.shape, jnp.float32).at[flat_ids]  2.5 us
    scatter x1, local copies, waits for them, and re-layouts, shards(): jnp.zeros((coefficients.shape[0],), jnp.float32).at[flat_ids]  2.45 us
  transfers between devices with their start and end apart: 5, of which 5 were waited for; matrix products, arithmetic and copies ran while one was open for 7% of the time, Pallas kernels for 0%

profile of v1, /device:TPU:24, one launch (start us, length us, event | category | flops | bytes accessed | tf_op | source)
XLA Modules:
  0.0 108.5 jit_solution(1053918347027110130)
XLA Ops:
  0.7 0.8 compare_select_fusion
  1.4 0.1 copy.16
  1.5 0.1 reshape.265
  1.6 0.7 fusion.26
  2.3 0.2 cosine_multiply_fusion.4
  2.5 0.1 copy.12
  2.6 0.1 broadcast_multiply_fusion.1
  2.7 0.1 reshape.288
  2.9 1.3 %fusion.6 = f32[8,8,32,128]{3,1,2,0:T(8,128)S(1)} fusion(bf16[1,64,4096]{2,1,0:T(8,128)(2,1)S(1)} %copy-done.1, f32[1,64,4096]{2,1,0:T(8,128)} %param.7), kind=kLoop, calls=%fused_computation.14 | loop fusion | flops 786432 | bytes 2621440
  4.2 0.2 copy.21
  4.4 1.7 %fusion.2 = f32[64,32,128]{2,0,1:T(8,128)S(1)} fusion(f32[128,128,1]{1,0,2:T(8,128)S(1)} %reshape.288, f32[64,32,128]{2,1,0:T(8,128)S(1)} %bitcast.56), kind=kOutput, calls=%fused_computation.7 | convolution fusion | flops 402653184 | bytes 2162688 | tf_op jit(solution)/shard_map/dot_general | solution.py:22
  6.0 1.2 %fusion.12 = f32[32,128,64]{1,2,0:T(8,128)S(1)} fusion(f32[64,32,128]{2,0,1:T(8,128)S(1)} %fusion.2, f32[64]{0:T(128)S(1)} %iota_convert_fusion, f32[64]{0:T(128)S(1)} %get-tuple-element.9, f32[64]{0:T(128)S(1)} %get-tuple-element.8), kind=kOutput, calls=%fused_computation.24 | convolution fusion | flops 201338880 | bytes 2097920 | tf_op jit(solution)/shard_map/kn,rnqj->rqkj/dot_general | solution.py:24
  7.3 1.0 gather_fusion
  8.3 0.1 broadcast_multiply_fusion
  8.4 25.6 %all_to_all.10 = f32[32,16,128]{2,1,0:T(8,128)S(1)} all-to-all(f32[32,16,128]{2,1,0:T(8,128)S(1)} %broadcast_multiply_fusion), channel_id=1, replica_groups=mesh['island'=16,'fsdp'=32] {'fsdp'}, dimensions={0} | all-to-all | bytes 524288 | tf_op jit(solution)/shard_map/all_to_all | solution.py:60
  34.1 2.0 %collective-permute-start = (f32[32,16,128]{2,1,0:T(8,128)S(1)}, f32[32,16,128]{2,1,0:T(8,128)S(1)}, u32[]{:S(2)}, u32[]{:S(2)}) collective-permute-start(f32[32,16,128]{2,1,0:T(8,128)S(1)} %all_to_all.10), channel_id=1, source_target_pairs={{0,32},{32,0},{64,96},{96,64},{128,160},{160,128},{192,224},{224,1... | collective-permute-start | bytes 786440 | tf_op jit(solution)/shard_map/ppermute | solution.py:44
  36.2 1.5 %collective-permute-done = f32[32,16,128]{2,1,0:T(8,128)S(1)} collective-permute-done((f32[32,16,128]{2,1,0:T(8,128)S(1)}, f32[32,16,128]{2,1,0:T(8,128)S(1)}, u32[]{:S(2)}, u32[]{:S(2)}) %collective-permute-start) | collective-permute-done | bytes 262176 | tf_op jit(solution)/shard_map/ppermute | solution.py:44
  37.7 2.4 %collective-permute-start.1 = (f32[32,16,128]{2,1,0:T(8,128)S(1)}, f32[32,16,128]{2,1,0:T(8,128)S(1)}, u32[]{:S(2)}, u32[]{:S(2)}) collective-permute-start(f32[32,16,128]{2,1,0:T(8,128)S(1)} %add.89), channel_id=1, source_target_pairs={{0,64},{32,96},{64,0},{96,32},{128,192},{160,224},{192,128},{224,1... | collective-permute-start | bytes 786440 | tf_op jit(solution)/shard_map/ppermute | solution.py:44
  40.1 0.1 copy.14
  40.1 0.1 reshape_squeeze.3
  40.2 7.7 %collective-permute-done.1 = f32[32,16,128]{2,1,0:T(8,128)S(1)} collective-permute-done((f32[32,16,128]{2,1,0:T(8,128)S(1)}, f32[32,16,128]{2,1,0:T(8,128)S(1)}, u32[]{:S(2)}, u32[]{:S(2)}) %collective-permute-start.1) | collective-permute-done | bytes 262176 | tf_op jit(solution)/shard_map/ppermute | solution.py:44
  48.0 2.2 %collective-permute-start.2 = (f32[32,16,128]{2,1,0:T(8,128)S(1)}, f32[32,16,128]{2,1,0:T(8,128)S(1)}, u32[]{:S(2)}, u32[]{:S(2)}) collective-permute-start(f32[32,16,128]{2,1,0:T(8,128)S(1)} %add.90), channel_id=1, source_target_pairs={{0,128},{32,160},{64,192},{96,224},{128,0},{160,32},{192,64},{224,... | collective-permute-start | bytes 786440 | tf_op jit(solution)/shard_map/ppermute | solution.py:44
  50.2 0.1 reshape.275
  50.3 0.1 mul.231
  50.4 2.4 %scatter_custom_fusion = f32[2048]{0:T(1024)S(1)} fusion(s32[512]{0:T(512)S(1)} %bitcast.60, f32[512]{0:T(512)S(1)} %reshape.275, f32[]{:T(128)} %constant.13.clone.1), kind=kCustom, calls=%fused_computation.46 | custom fusion | bytes 8196 | tf_op jit(solution)/shard_map/scatter | solution.py:64
  52.9 0.1 mul.237
  53.0 1.3 %convolution_bitcast_fusion.1 = f32[1,64,32,128]{3,1,2,0:T(8,128)S(1)} fusion(f32[32,128,64]{1,2,0:T(8,128)S(1)} %fusion.12, f32[32,64]{1,0:T(8,128)S(1)} %mul.237, f32[64]{0:T(128)S(1)} %iota_convert_fusion, f32[64]{0:T(128)S(1)} %get-tuple-element.9, f32[64]{0:T(128)S(1)} %get-tuple-element.8), kind=kOutput, calls=%fused_computation.4 | convolution fusion | flops 201601024 | bytes 2106112 | tf_op jit(solution)/shard_map/kn,rqkj->rnqj/dot_general | solution.py:31
  54.3 0.6 copy.15
  54.9 8.9 %collective-permute-done.2 = f32[32,16,128]{2,1,0:T(8,128)S(1)} collective-permute-done((f32[32,16,128]{2,1,0:T(8,128)S(1)}, f32[32,16,128]{2,1,0:T(8,128)S(1)}, u32[]{:S(2)}, u32[]{:S(2)}) %collective-permute-start.2) | collective-permute-done | bytes 262176 | tf_op jit(solution)/shard_map/ppermute | solution.py:44
  63.8 5.2 %collective-permute-start.3 = (f32[32,16,128]{2,1,0:T(8,128)S(1)}, f32[32,16,128]{2,1,0:T(8,128)S(1)}, u32[]{:S(2)}, u32[]{:S(2)}) collective-permute-start(f32[32,16,128]{2,1,0:T(8,128)S(1)} %add.91), channel_id=1, source_target_pairs={{0,256},{32,288},{64,320},{96,352},{128,384},{160,416},{192,448},{... | collective-permute-start | bytes 786440 | tf_op jit(solution)/shard_map/ppermute | solution.py:44
  69.0 1.0 fusion.32
  70.0 0.2 reshape.256
  70.2 0.0 copy-start
  70.2 12.3 %collective-permute-done.3 = f32[32,16,128]{2,1,0:T(8,128)S(1)} collective-permute-done((f32[32,16,128]{2,1,0:T(8,128)S(1)}, f32[32,16,128]{2,1,0:T(8,128)S(1)}, u32[]{:S(2)}, u32[]{:S(2)}) %collective-permute-start.3) | collective-permute-done | bytes 262176 | tf_op jit(solution)/shard_map/ppermute | solution.py:44
  82.5 0.1 multiply_reduce_fusion
  82.6 0.8 broadcast_divide_fusion
  83.5 4.3 %all-to-all-start.1 = ((f32[32,16,128]{2,1,0:T(8,128)}), f32[32,16,128]{2,1,0:T(8,128)S(1)}, u32[]{:S(2)}, u32[]{:S(2)}) async-start(f32[32,16,128]{2,1,0:T(8,128)} %broadcast_divide_fusion), calls=%async_computation.1 | async-start | bytes 524288 | tf_op jit(solution)/shard_map/all_to_all | solution.py:62
  87.8 1.1 %fusion.5 = f32[1,64,4096]{2,1,0:T(8,128)} fusion(f32[1,64,4096]{2,1,0:T(8,128)S(1)} %reshape.256, bf16[1,64,4096]{2,1,0:T(8,128)(2,1)S(1)} %copy-done.1, f32[1,64,4096]{2,1,0:T(8,128)S(1)} %copy-done), kind=kLoop, calls=%fused_computation.13 | loop fusion | flops 1048576 | bytes 3670016 | tf_op jit(solution)/shard_map/sub | solution.py:66
  88.9 0.8 fusion.41
  89.7 10.9 %all-to-all-done.1 = f32[32,16,128]{2,1,0:T(8,128)S(1)} async-done(((f32[32,16,128]{2,1,0:T(8,128)}), f32[32,16,128]{2,1,0:T(8,128)S(1)}, u32[]{:S(2)}, u32[]{:S(2)}) %all-to-all-start.1) | async-done | bytes 262176 | tf_op jit(solution)/shard_map/all_to_all | solution.py:62
  100.6 2.5 %scatter_custom_fusion.1 = f32[2048,128]{1,0:T(8,128)S(1)} fusion(s32[512]{0:T(512)S(1)} %bitcast.61, f32[512,128]{1,0:T(8,128)S(1)} %bitcast.59, f32[]{:T(128)} %constant.13.clone.1), kind=kCustom, calls=%fused_computation.15 | custom fusion | flops 65536 | bytes 1048580 | tf_op jit(solution)/shard_map/scatter-add | solution.py:70
  103.1 1.3 %convolution_bitcast_fusion = f32[1,64,32,128]{3,1,2,0:T(8,128)S(1)} fusion(f32[32,64,128]{2,1,0:T(8,128)S(1)} %bitcast.55, f32[64]{0:T(128)S(1)} %iota_convert_fusion, f32[64]{0:T(128)S(1)} %get-tuple-element.9, f32[64]{0:T(128)S(1)} %get-tuple-element.8), kind=kOutput, calls=%fused_computation.3 | convolution fusion | flops 201338880 | bytes 2097920 | tf_op jit(solution)/shard_map/kn,rqkj->rnqj/dot_general | solution.py:31
  104.4 0.6 copy.17
  105.0 1.0 fusion.33
  106.0 0.2 reshape.261
  106.2 0.8 copy-done.2
  107.1 0.2 copy-done.3
  107.2 1.3 %fusion.4 = (bf16[64,4096]{1,0:T(8,128)(2,1)}, bf16[64,4096]{1,0:T(8,128)(2,1)}) fusion(f32[64,4096]{1,0:T(8,128)S(1)} %reshape.261, bf16[64,4096]{1,0:T(8,128)(2,1)S(1)} %copy-done.2, bf16[64,4096]{1,0:T(8,128)(2,1)S(1)} %copy-done.3), kind=kLoop, calls=%fused_computation.11 | loop fusion | flops 2621440 | bytes 3145728 | tf_op jit(solution)/shard_map/convert_element_type | solution.py:74
  (16 shorter events, 0.2 us)
Async XLA Ops:
  0.6 2.2 %copy-start.1 = (bf16[1,64,4096]{2,1,0:T(8,128)(2,1)S(1)}, bf16[1,64,4096]{2,1,0:T(8,128)(2,1)}, u32[]{:S(2)}) copy-start(bf16[1,64,4096]{2,1,0:T(8,128)(2,1)} %param.6) | copy-start | bytes 1572868
  34.1 6.0 %copy-start.4 = (s32[1,32,16]{1,2,0:T(8,128)S(1)}, s32[1,32,16]{1,2,0:T(8,128)}, u32[]{:S(2)}) copy-start(s32[1,32,16]{1,2,0:T(8,128)} %param.10) | copy-start | bytes 6148
  34.1 3.5 %collective-permute-start = (f32[32,16,128]{2,1,0:T(8,128)S(1)}, f32[32,16,128]{2,1,0:T(8,128)S(1)}, u32[]{:S(2)}, u32[]{:S(2)}) collective-permute-start(f32[32,16,128]{2,1,0:T(8,128)S(1)} %all_to_all.10), channel_id=1, source_target_pairs={{0,32},{32,0},{64,96},{96,64},{128,160},{160,128},{192,224},{224,1... | collective-permute-start | bytes 786440 | tf_op jit(solution)/shard_map/ppermute | solution.py:44
  37.7 10.2 %collective-permute-start.1 = (f32[32,16,128]{2,1,0:T(8,128)S(1)}, f32[32,16,128]{2,1,0:T(8,128)S(1)}, u32[]{:S(2)}, u32[]{:S(2)}) collective-permute-start(f32[32,16,128]{2,1,0:T(8,128)S(1)} %add.89), channel_id=1, source_target_pairs={{0,64},{32,96},{64,0},{96,32},{128,192},{160,224},{192,128},{224,1... | collective-permute-start | bytes 786440 | tf_op jit(solution)/shard_map/ppermute | solution.py:44
  48.0 15.8 %collective-permute-start.2 = (f32[32,16,128]{2,1,0:T(8,128)S(1)}, f32[32,16,128]{2,1,0:T(8,128)S(1)}, u32[]{:S(2)}, u32[]{:S(2)}) collective-permute-start(f32[32,16,128]{2,1,0:T(8,128)S(1)} %add.90), channel_id=1, source_target_pairs={{0,128},{32,160},{64,192},{96,224},{128,0},{160,32},{192,64},{224,... | collective-permute-start | bytes 786440 | tf_op jit(solution)/shard_map/ppermute | solution.py:44
  63.8 18.7 %collective-permute-start.3 = (f32[32,16,128]{2,1,0:T(8,128)S(1)}, f32[32,16,128]{2,1,0:T(8,128)S(1)}, u32[]{:S(2)}, u32[]{:S(2)}) collective-permute-start(f32[32,16,128]{2,1,0:T(8,128)S(1)} %add.91), channel_id=1, source_target_pairs={{0,256},{32,288},{64,320},{96,352},{128,384},{160,416},{192,448},{... | collective-permute-start | bytes 786440 | tf_op jit(solution)/shard_map/ppermute | solution.py:44
  70.2 17.6 %copy-start = (f32[1,64,4096]{2,1,0:T(8,128)S(1)}, f32[1,64,4096]{2,1,0:T(8,128)}, u32[]{:S(2)}) copy-start(f32[1,64,4096]{2,1,0:T(8,128)} %param.7) | copy-start | bytes 3145732
  83.5 17.1 %all-to-all-start.1 = ((f32[32,16,128]{2,1,0:T(8,128)}), f32[32,16,128]{2,1,0:T(8,128)S(1)}, u32[]{:S(2)}, u32[]{:S(2)}) async-start(f32[32,16,128]{2,1,0:T(8,128)} %broadcast_divide_fusion), calls=%async_computation.1 | async-start | bytes 524288 | tf_op jit(solution)/shard_map/all_to_all | solution.py:62
  106.0 1.0 copy-start.2
  106.0 1.2 %copy-start.3 = (bf16[64,4096]{1,0:T(8,128)(2,1)S(1)}, bf16[64,4096]{1,0:T(8,128)(2,1)}, u32[]{:S(2)}) copy-start(bf16[64,4096]{1,0:T(8,128)(2,1)} %param.8) | copy-start | bytes 1572868
